TPU v7x, 32 devices: a whole 2x2x4 slice. The times are simulated.
32 devices in a mesh: groups: 2 (over y), dp: 4 (over z), mp: 2 (over x), role: 2 (over core).
Axes of the slice: x: 2, y: 2, z: 4, core: 2. Of those that a mesh axis runs over, the one named last changes fastest.
Arguments:
- train_x: bfloat16 [4096, 8192], P(('groups', 'dp', 'role'), 'mp'), parts along dimension 0, may hold values from -6 to 6
- train_cot: bfloat16 [4096, 4096], P(('groups', 'dp', 'role'), 'mp'), parts along dimension 0, may hold values from -6 to 6
- tenant_of_block: int32 [32], P(('groups', 'dp', 'role')), parts along dimension 0, may hold values from 0 to 7
- down_factors: float32 [512, 8192], P(('groups', 'dp', 'role'), 'mp'), parts along dimension 0, may hold values from -0.0625 to 0.0625
- up_factors: float32 [512, 4096], P(('groups', 'dp', 'role'), 'mp'), parts along dimension 0, may hold values from -1 to 1
- down_mean_moment: float32 [512, 8192], P(('groups', 'dp', 'role'), 'mp'), parts along dimension 0, may hold values from -120 to 120
- down_square_moment: float32 [512, 8192], P(('groups', 'dp', 'role'), 'mp'), parts along dimension 0, may hold values from 100 to 10000
- up_mean_moment: float32 [512, 4096], P(('groups', 'dp', 'role'), 'mp'), parts along dimension 0, may hold values from -120 to 120
- up_square_moment: float32 [512, 4096], P(('groups', 'dp', 'role'), 'mp'), parts along dimension 0, may hold values from 100 to 10000
- base_weight: bfloat16 [8192, 4096], P('mp', ('dp', 'role')), may hold values from -0.0625 to 0.0625
- base_scale: bfloat16 [128, 4096], P('mp', ('dp', 'role')), may hold values from 0.5 to 2
- row_hidden: bfloat16 [32, 8192], P(('groups', 'dp', 'role')), parts along dimension 0, may hold values from -6 to 6
- row_tenant: int32 [32], P(('groups', 'dp', 'role')), parts along dimension 0, may hold values from 0 to 7
- cache_len: int32 [32], P(('groups', 'dp', 'role')), parts along dimension 0, may hold values from 1 to 1024, as said below
- kv_cache: bfloat16 [32, 8, 1024, 256], P(('groups', 'dp', 'role'), 'mp'), parts along dimension 0, may hold values from -2000 to 2000
- new_kv: bfloat16 [32, 8, 256], P(('groups', 'dp', 'role'), 'mp'), parts along dimension 0, may hold values from -6 to 6
Outputs:
- down_direction: float32 [512, 8192], P(('groups', 'dp', 'role'), 'mp'), parts along dimension 0
- up_direction: float32 [512, 4096], P(('groups', 'dp', 'role'), 'mp'), parts along dimension 0
- training_input_gradient: bfloat16 [4096, 8192], P(('groups', 'dp', 'role'), 'mp'), parts along dimension 0
- attended: bfloat16 [32, 4096], P(('groups', 'dp', 'role'), 'mp'), parts along dimension 0
There are 2 independent parts, one for each index of `groups`. A program takes and returns all parts, laid end to end along the dimension named above; an argument that names none is the same for every part. Nothing has to cross between parts.
Inputs may be any that keep to these rules, and one draw needn't show every extreme that they name: `cache_len`: some row has exactly 1024 valid positions.
All inputs are finite; a program needn't handle non-finite values.
Results may differ from a plain program's by a relative error of at most 0.007.
Values may be sent and summed in bfloat16 or wider, within the bound.
No kernel may reach another device: no remote copies, remote signals or barrier semaphores. Data moves between devices by JAX's collectives and lax.ppermute only.
A program may use at most 192 MiB of HBM per device.

v0:
```python
import math

import jax
import jax.numpy as jnp
from jax import lax
from jax.sharding import PartitionSpec as P

HEAD_DIM = 128
ADAPTER_RANK = 32
TENANT_COUNT = 8
GROUP = 64
BLOCK = 128


ADAPTER_SCALE = 2.0
FIRST_DECAY = 0.9
SECOND_DECAY = 0.999
FIRST_CORR = 1.0 / (1.0 - 0.9**10)
SECOND_CORR = 1.0 / (1.0 - 0.999**10)
ADAM_EPS = 1e-08
STEP_RATE = 0.002
TOP_PRECISION = lax.Precision.HIGHEST


def dequantize(base_weight, base_scale):
    spread = jnp.repeat(base_scale.astype(jnp.float32), GROUP, axis=0)
    return (base_weight.astype(jnp.float32) * spread).astype(jnp.bfloat16)


def moment_step_update(master, gradient, first, second):
    first_new = FIRST_DECAY * first + (1.0 - FIRST_DECAY) * gradient
    second_new = SECOND_DECAY * second + (1.0 - SECOND_DECAY) * gradient * gradient
    update = first_new * FIRST_CORR / (jnp.sqrt(second_new * SECOND_CORR) + ADAM_EPS)
    return (update, master - STEP_RATE * update)


def attend(query_vector, kv_cache, new_kv, cache_len):
    row_count = query_vector.shape[0]
    heads_kv = kv_cache.shape[1]
    positions = kv_cache.shape[2]
    grouped = query_vector.reshape(row_count, heads_kv, -1, HEAD_DIM)
    keys = kv_cache[..., :HEAD_DIM]
    values = kv_cache[..., HEAD_DIM:]
    inverse = 1.0 / math.sqrt(HEAD_DIM)
    scores = (
        jnp.einsum("bkgh,bkph->bkgp", grouped, keys, preferred_element_type=jnp.float32) * inverse
    )
    own = (
        jnp.einsum(
            "bkgh,bkh->bkg", grouped, new_kv[..., :HEAD_DIM], preferred_element_type=jnp.float32
        )
        * inverse
    )
    live = (jnp.arange(positions, dtype=jnp.int32)[None, :] < cache_len[:, None])[:, None, None, :]
    top = jnp.maximum(jnp.max(jnp.where(live, scores, -jnp.inf), axis=-1), own)
    expo = jnp.where(live, jnp.exp(scores - top[..., None]), 0.0)
    own_expo = jnp.exp(own - top)
    total = jnp.sum(expo, axis=-1) + own_expo
    weights = (expo / total[..., None]).astype(jnp.bfloat16)
    own_weight = (own_expo / total).astype(jnp.bfloat16)
    own_value = new_kv[..., HEAD_DIM:].astype(jnp.float32)
    mixed = jnp.einsum("bkgp,bkph->bkgh", weights, values, preferred_element_type=jnp.float32)
    mixed = mixed + own_weight.astype(jnp.float32)[..., None] * own_value[:, :, None, :]
    return mixed.astype(jnp.bfloat16).reshape(row_count, -1)


def local(
    train_x,
    train_cot,
    tenant_of_block,
    down_factors,
    up_factors,
    down_mean_moment,
    down_square_moment,
    up_mean_moment,
    up_square_moment,
    base_weight,
    base_scale,
    row_hidden,
    row_tenant,
    cache_len,
    kv_cache,
    new_kv,
):
    token_rows, model_local = train_x.shape
    query_local = train_cot.shape[1]
    block_count = token_rows // BLOCK
    tenant_ids = jnp.arange(TENANT_COUNT, dtype=jnp.int32)
    current_down, current_up = (
        lax.all_gather(down_factors.astype(jnp.bfloat16), ("dp", "role"), axis=0, tiled=True),
        lax.all_gather(up_factors.astype(jnp.bfloat16), ("dp", "role"), axis=0, tiled=True),
    )
    block_onehot = (tenant_of_block[:, None] == tenant_ids[None, :]).astype(jnp.float32)
    block_pick = block_onehot.astype(jnp.bfloat16)
    block_down = jnp.einsum(
        "bt,trd->brd",
        block_pick,
        current_down.reshape(TENANT_COUNT, ADAPTER_RANK, model_local),
        preferred_element_type=jnp.float32,
    ).astype(jnp.bfloat16)
    block_up = jnp.einsum(
        "bt,trc->brc",
        block_pick,
        current_up.reshape(TENANT_COUNT, ADAPTER_RANK, query_local),
        preferred_element_type=jnp.float32,
    ).astype(jnp.bfloat16)
    input_blocks = train_x.reshape(block_count, BLOCK, model_local)
    cotangent_blocks = train_cot.reshape(block_count, BLOCK, query_local)
    down_terms = jnp.einsum(
        "bjd,brd->bjr", input_blocks, block_down, preferred_element_type=jnp.float32
    )
    up_terms = jnp.einsum(
        "bjc,brc->bjr", cotangent_blocks, block_up, preferred_element_type=jnp.float32
    )
    down_total, up_total = lax.psum((down_terms, up_terms), "mp")
    u_low = down_total.astype(jnp.bfloat16)
    gradient_lowrank = up_total.astype(jnp.bfloat16)
    down_gradient_blocks = jnp.einsum(
        "bjr,bjd->brd", gradient_lowrank, input_blocks, preferred_element_type=jnp.float32
    )
    up_gradient_blocks = jnp.einsum(
        "bjr,bjc->brc", u_low, cotangent_blocks, preferred_element_type=jnp.float32
    )
    dense_down = jnp.einsum(
        "eg,eql->gql", block_onehot, down_gradient_blocks, precision=TOP_PRECISION
    ).reshape(TENANT_COUNT * ADAPTER_RANK, model_local)
    dense_up = jnp.einsum(
        "uv,uny->vny", block_onehot, up_gradient_blocks, precision=TOP_PRECISION
    ).reshape(TENANT_COUNT * ADAPTER_RANK, query_local)
    down_gradient, up_gradient = (
        lax.psum_scatter(dense_down, ("dp", "role"), scatter_dimension=0, tiled=True),
        lax.psum_scatter(dense_up, ("dp", "role"), scatter_dimension=0, tiled=True),
    )
    down_direction, revised_down = moment_step_update(
        down_factors, ADAPTER_SCALE * down_gradient, down_mean_moment, down_square_moment
    )
    up_direction, revised_up = moment_step_update(
        up_factors, ADAPTER_SCALE * up_gradient, up_mean_moment, up_square_moment
    )
    adapter_input = jnp.einsum(
        "bjr,brd->bjd", gradient_lowrank, block_down, preferred_element_type=jnp.float32
    ).reshape(token_rows, model_local)
    slice_start = lax.axis_index("mp") * model_local
    hidden_local = lax.dynamic_slice_in_dim(row_hidden, slice_start, model_local, 1)
    cot_every = lax.all_gather(train_cot, "mp", axis=1, tiled=True)
    piece = dequantize(
        lax.all_gather(base_weight, ("dp", "role"), axis=1, tiled=True),
        lax.all_gather(base_scale, ("dp", "role"), axis=1, tiled=True),
    )
    grad_terms = jnp.einsum("tc,dc->td", cot_every, piece, preferred_element_type=jnp.float32)
    columns = jnp.dot(hidden_local, piece, preferred_element_type=jnp.float32)
    query_terms = columns
    frozen_input_gradient, query_terms = (grad_terms, query_terms)
    frozen_query = lax.psum_scatter(query_terms, "mp", scatter_dimension=1, tiled=True)
    training_input_gradient = (frozen_input_gradient + ADAPTER_SCALE * adapter_input).astype(
        jnp.bfloat16
    )
    fresh_down = revised_down.astype(jnp.bfloat16)
    fresh_up = revised_up.astype(jnp.bfloat16)
    every_down, every_up = (
        lax.all_gather(fresh_down, ("dp", "role"), axis=0, tiled=True),
        lax.all_gather(fresh_up, ("dp", "role"), axis=0, tiled=True),
    )
    row_pick = (row_tenant[:, None] == tenant_ids[None, :]).astype(jnp.bfloat16)
    row_down = jnp.einsum(
        "bt,trd->brd",
        row_pick,
        every_down.reshape(TENANT_COUNT, ADAPTER_RANK, model_local),
        preferred_element_type=jnp.float32,
    ).astype(jnp.bfloat16)
    row_up = jnp.einsum(
        "bt,trc->brc",
        row_pick,
        every_up.reshape(TENANT_COUNT, ADAPTER_RANK, query_local),
        preferred_element_type=jnp.float32,
    ).astype(jnp.bfloat16)
    rank_terms = jnp.einsum(
        "bd,brd->br", hidden_local, row_down, preferred_element_type=jnp.float32
    )
    rank_total = lax.psum(rank_terms, "mp")
    adapter_difference = jnp.einsum(
        "br,brc->bc", rank_total.astype(jnp.bfloat16), row_up, preferred_element_type=jnp.float32
    )
    query_vector = (frozen_query + ADAPTER_SCALE * adapter_difference).astype(jnp.bfloat16)
    attended = attend(query_vector, kv_cache, new_kv, cache_len)
    return (down_direction, up_direction, training_input_gradient, attended)


def solution(mesh):
    in_specs = (
        P(("groups", "dp", "role"), "mp"),
        P(("groups", "dp", "role"), "mp"),
        P(("groups", "dp", "role")),
        P(("groups", "dp", "role"), "mp"),
        P(("groups", "dp", "role"), "mp"),
        P(("groups", "dp", "role"), "mp"),
        P(("groups", "dp", "role"), "mp"),
        P(("groups", "dp", "role"), "mp"),
        P(("groups", "dp", "role"), "mp"),
        P("mp", ("dp", "role")),
        P("mp", ("dp", "role")),
        P(("groups", "dp", "role"), None),
        P(("groups", "dp", "role")),
        P(("groups", "dp", "role")),
        P(("groups", "dp", "role"), "mp", None, None),
        P(("groups", "dp", "role"), "mp", None),
    )
    out_specs = (
        P(("groups", "dp", "role"), "mp"),
        P(("groups", "dp", "role"), "mp"),
        P(("groups", "dp", "role"), "mp"),
        P(("groups", "dp", "role"), "mp"),
    )
    return jax.shard_map(local, mesh=mesh, in_specs=in_specs, out_specs=out_specs, check_vma=False)
```

profile of v0, /device:TPU:0, one launch (start us, length us, event | category | flops | bytes accessed | tf_op | source)
XLA Modules:
  0.0 616.7 jit_solution(7250445675104268679)
XLA Ops:
  9.1 26.0 %all-gather.7.cloned.1.call-done = bf16[256,2048]{1,0:T(8,128)(2,1)} async-done(((bf16[32,2048]{1,0:T(8,128)(2,1)}), bf16[256,2048]{1,0:T(8,128)(2,1)}) %all-gather.7.cloned.1.call-update) | async-done | bytes 1048592 | tf_op jit(solution)/shard_map/all_gather | solution.py:91
  35.0 2.1 convolution_convert_fusion.3
  38.8 8.3 %psum.21 = bf16[2,128,32]{1,2,0:T(8,128)(2,1)S(1)} all-reduce(f32[2,128,32]{1,2,0:T(8,128)S(1)} %convolution_bitcast_fusion.2), channel_id=1, replica_groups=mesh['groups'=2,'dp'=4,'mp'=2,'role'=2] {'mp'}, use_global_device_ids=true, to_apply=%region_0.0 | all-reduce | flops 8192 | bytes 49152 | tf_op jit(solution)/shard_map/psum | solution.py:115
  47.5 3.0 fusion.19
  50.5 4.4 copy.42
  55.0 48.8 %reduce-scatter.6.cloned.1.call-done = f32[32,4096]{1,0:T(8,128)} async-done(((f32[256,4096]{1,0:T(8,128)}), f32[32,4096]{1,0:T(8,128)}) %reduce-scatter.6.cloned.1.call-update) | async-done | bytes 524304 | tf_op jit(solution)/shard_map/reduce_scatter | solution.py:131
  103.8 2.6 subtract_convert_fusion
  107.2 26.6 %all-gather.9.cloned.1.call-done = bf16[256,4096]{1,0:T(8,128)(2,1)} async-done(((bf16[32,4096]{1,0:T(8,128)(2,1)}), bf16[256,4096]{1,0:T(8,128)(2,1)}) %all-gather.9.cloned.1.call-update) | async-done | bytes 2097168 | tf_op jit(solution)/shard_map/all_gather | solution.py:90
  133.8 4.1 convolution_convert_fusion.1
  138.7 25.7 %all-gather.15.cloned.1.call-done = bf16[256,4096]{1,0:T(8,128)(2,1)} async-done(((bf16[32,4096]{1,0:T(8,128)(2,1)}), bf16[256,4096]{1,0:T(8,128)(2,1)}) %all-gather.15.cloned.1.call-update) | async-done | bytes 2097168 | tf_op jit(solution)/shard_map/all_gather | solution.py:161
  164.4 4.1 convolution_convert_fusion
  168.9 8.4 %all-reduce = (bf16[2,128,32]{1,2,0:T(8,128)(2,1)S(1)}, bf16[2,32]{1,0:T(2,128)(2,1)S(1)}) all-reduce(f32[2,128,32]{1,2,0:T(8,128)S(1)} %convolution_bitcast_fusion.3, f32[2,32]{1,0:T(2,128)S(1)} %bitcast.84), channel_id=1, replica_groups=mesh['groups'=2,'dp'=4,'mp'=2,'role'=2] {'mp'}, use_global_device_ids=true, to_apply=%region_2.0 | all-reduce | flops 8256 | bytes 49536 | tf_op jit(solution)/shard_map/psum | solution.py:115
  179.2 2.5 copy.46
  181.8 34.5 %reduce-scatter.8.cloned.1.call-done = f32[32,2048]{1,0:T(8,128)} async-done(((f32[256,2048]{1,0:T(8,128)}), f32[32,2048]{1,0:T(8,128)}) %reduce-scatter.8.cloned.1.call-update) | async-done | bytes 262160 | tf_op jit(solution)/shard_map/reduce_scatter | solution.py:132
  219.9 15.8 %all_gather.24 = bf16[64,4096]{1,0:T(8,128)(2,1)S(1)} all-gather(bf16[64,512]{1,0:T(8,128)(2,1)S(1)} %copy-done.8), channel_id=1, replica_groups=mesh['groups'=2,'dp'=4,'mp'=2,'role'=2] {'dp','role'}, dimensions={1}, use_global_device_ids=true | all-gather | bytes 589824 | tf_op jit(solution)/shard_map/all_gather | solution.py:148
  235.8 3.1 convolution_multiply_fusion
  238.9 5.6 copy.60
  246.8 284.2 %all-gather.11.cloned.1.call-done = bf16[4096,4096]{1,0:T(8,128)(2,1)} async-done(((bf16[4096,512]{1,0:T(8,128)(2,1)}), bf16[4096,4096]{1,0:T(8,128)(2,1)}) %all-gather.11.cloned.1.call-update) | async-done | bytes 33554448 | tf_op jit(solution)/shard_map/all_gather | solution.py:147
  531.0 23.7 %fusion = bf16[4096,4096]{1,0:T(8,128)(2,1)} fusion(bf16[4096,4096]{1,0:T(8,128)(2,1)} %all-gather.11.cloned.1.call-done, f32[64,4096]{1,0:T(8,128)S(1)} %convert_element_type.79), kind=kLoop, calls=%fused_computation.1 | loop fusion | flops 50331648 | bytes 68157440 | tf_op jit(solution)/shard_map/convert_element_type | solution.py:27
  554.7 18.2 %convolution_bitcast_fusion.1 = f32[4096,2]{1,0:T(8,128)} fusion(bf16[4096,4096]{1,0:T(8,128)(2,1)} %fusion, bf16[2,8192]{1,0:T(2,128)(2,1)S(1)} %copy-done.9, s32[]{:T(128)S(6)} %select_n.10), kind=kOutput, calls=%fused_computation.6 | convolution fusion | flops 67108864 | bytes 33603588
  573.0 17.8 %fusion.2 = bf16[256,4096]{0,1:T(8,128)(2,1)S(1)} fusion(f32[256,4096]{0,1:T(8,128)} %copy.60, bf16[4096,4096]{1,0:T(8,128)(2,1)} %fusion, bf16[256,4096]{1,0:T(8,128)(2,1)} %all-gather.13.cloned.1.call-done), kind=kOutput, calls=%fused_computation.5 | convolution fusion | flops 8592031744 | bytes 41943040 | tf_op jit(solution)/shard_map/tc,dc->td/dot_general | solution.py:150
  590.8 2.9 copy.51
  593.7 9.4 %reduce-scatter.10.cloned.1.call-done = f32[2048,2]{1,0:T(8,128)} async-done(((f32[4096,2]{1,0:T(8,128)}), f32[2048,2]{1,0:T(8,128)}) %reduce-scatter.10.cloned.1.call-update) | async-done | bytes 16400
  604.8 2.5 select_reduce_fusion
  (71 shorter events, 18.5 us)
Async XLA Ops:
  7.2 39.9 %copy-start = (bf16[256,4096]{1,0:T(8,128)(2,1)S(1)}, bf16[256,4096]{1,0:T(8,128)(2,1)}, u32[]{:S(2)}) copy-start(bf16[256,4096]{1,0:T(8,128)(2,1)} %param.16) | copy-start | bytes 6291460
  7.2 27.8 %all-gather.7.cloned.1.call-start = ((), (), s32[]{:S(2)}) async-start(), calls=%async_computation.3 | async-start | bytes 1179648 | tf_op jit(solution)/shard_map/all_gather | solution.py:91
  9.0 94.8 %reduce-scatter.6.cloned.1.call-start = ((), (), s32[]{:S(2)}) async-start(), calls=%async_computation.4 | async-start | bytes 4718592 | tf_op jit(solution)/shard_map/reduce_scatter | solution.py:131
  37.1 10.4 %copy-start.10 = (s32[2]{0:T(128)S(1)}, s32[2]{0:T(128)}, u32[]{:S(2)}) copy-start(s32[2]{0:T(128)} %param.18) | copy-start | bytes 28
  54.9 48.9 %copy-start.4 = (f32[32,4096]{1,0:T(8,128)S(1)}, f32[32,4096]{1,0:T(8,128)}, u32[]{:S(2)}) copy-start(f32[32,4096]{1,0:T(8,128)} %param.19) | copy-start | bytes 1572868
  54.9 48.9 %copy-start.5 = (f32[32,4096]{1,0:T(8,128)S(1)}, f32[32,4096]{1,0:T(8,128)}, u32[]{:S(2)}) copy-start(f32[32,4096]{1,0:T(8,128)} %param.22) | copy-start | bytes 1572868
  54.9 52.3 %copy-start.9 = (bf16[2,8192]{1,0:T(2,128)(2,1)S(1)}, bf16[2,8192]{1,0:T(2,128)(2,1)}, u32[]{:S(2)}) copy-start(bf16[2,8192]{1,0:T(2,128)(2,1)} %param.27) | copy-start | bytes 98308
  54.9 78.9 %all-gather.9.cloned.1.call-start = ((), (), s32[]{:S(2)}) async-start(), calls=%async_computation.5 | async-start | bytes 2359296 | tf_op jit(solution)/shard_map/all_gather | solution.py:90
  106.4 58.1 %all-gather.15.cloned.1.call-start = ((), (), s32[]{:S(2)}) async-start(), calls=%async_computation.9 | async-start | bytes 2359296 | tf_op jit(solution)/shard_map/all_gather | solution.py:161
  106.9 109.4 %reduce-scatter.8.cloned.1.call-start = ((), (), s32[]{:S(2)}) async-start(), calls=%async_computation.6 | async-start | bytes 2359296 | tf_op jit(solution)/shard_map/reduce_scatter | solution.py:132
  133.8 30.7 %copy-start.12 = (s32[2]{0:T(128)S(1)}, s32[2]{0:T(128)}, u32[]{:S(2)}) copy-start(s32[2]{0:T(128)} %param.28) | copy-start | bytes 28
  138.7 38.7 %copy-start.2 = (bf16[256,2048]{1,0:T(8,128)(2,1)S(1)}, bf16[256,2048]{1,0:T(8,128)(2,1)}, u32[]{:S(2)}) copy-start(bf16[256,2048]{1,0:T(8,128)(2,1)} %param.17) | copy-start | bytes 3145732
  181.7 34.6 %copy-start.3 = (f32[32,2048]{1,0:T(8,128)S(1)}, f32[32,2048]{1,0:T(8,128)}, u32[]{:S(2)}) copy-start(f32[32,2048]{1,0:T(8,128)} %param.20) | copy-start | bytes 786436
  181.8 34.6 %copy-start.6 = (f32[32,2048]{1,0:T(8,128)S(1)}, f32[32,2048]{1,0:T(8,128)}, u32[]{:S(2)}) copy-start(f32[32,2048]{1,0:T(8,128)} %param.24) | copy-start | bytes 786436
  181.8 34.6 %copy-start.7 = (f32[32,2048]{1,0:T(8,128)S(1)}, f32[32,2048]{1,0:T(8,128)}, u32[]{:S(2)}) copy-start(f32[32,2048]{1,0:T(8,128)} %param.23) | copy-start | bytes 786436
  181.8 62.7 %all-gather.17.cloned.1.call-start = ((), (), s32[]{:S(2)}) async-start(), calls=%async_computation.10 | async-start | bytes 1179648 | tf_op jit(solution)/shard_map/all_gather | solution.py:162
  218.3 1.6 copy-start.8
  218.3 312.7 %all-gather.11.cloned.1.call-start = ((), (), s32[]{:S(2)}) async-start(), calls=%async_computation.7 | async-start | bytes 37748736 | tf_op jit(solution)/shard_map/all_gather | solution.py:147
  219.0 16.7 %copy-start.13 = (s32[2]{0:T(128)S(1)}, s32[2]{0:T(128)}, u32[]{:S(2)}) copy-start(s32[2]{0:T(128)} %param.29) | copy-start | bytes 28
  219.0 16.8 %copy-start.11 = (bf16[2,4,256]{2,1,0:T(4,128)(2,1)S(1)}, bf16[2,4,256]{2,1,0:T(4,128)(2,1)}, u32[]{:S(2)}) copy-start(bf16[2,4,256]{2,1,0:T(4,128)(2,1)} %param.31) | copy-start | bytes 12292
  219.0 353.9 %all-gather.13.cloned.1.call-start = ((), (), s32[]{:S(2)}) async-start(), calls=%async_computation.8 | async-start | bytes 3145728 | tf_op jit(solution)/shard_map/all_gather | solution.py:145
  219.8 383.3 %reduce-scatter.10.cloned.1.call-start = ((), (), s32[]{:S(2)}) async-start(), calls=%async_computation.11 | async-start | bytes 3145728
  604.8 5.4 copy-start.1
Sparse Core Ops, SparseCore 0:
  10.2 24.7 all-gather.6
  55.0 48.7 reduce-scatter.5
  106.5 27.2 all-gather.8
  135.8 28.5 all-gather.14
  181.9 34.3 reduce-scatter.7
  218.4 22.7 all-gather.16
  242.8 288.1 all-gather.10
  532.5 31.2 all-gather.12
  573.1 29.9 reduce-scatter.9
where the time goes:
time: 617 us
  waiting for transfers between devices  457 us (74%)
  matrix products  64.4 us (10%)
  blocking collectives  32.5 us (5%)
  other arithmetic  30.3 us (5%)
  local copies, waits for them, and re-layouts  17.7 us (3%)
  between operations  14 us (2%)
    all_gather x1, waiting for transfers between devices, local(): lax.all_gather(base_weight, ('dp', 'role'), axis=1, tiled=True)  284 us
    reduce_scatter x1, waiting for transfers between devices, local(): lax.psum_scatter(dense_down, ('dp', 'role'), scatter_dimension=0, tiled=T...  48.8 us
    reduce_scatter x1, waiting for transfers between devices, local(): lax.psum_scatter(dense_up, ('dp', 'role'), scatter_dimension=0, tiled=True)  34.5 us
    all_gather x1, waiting for transfers between devices, local(): lax.all_gather(down_factors.astype(jnp.bfloat16), ('dp', 'role'), axis=0,...  26.6 us
    all_gather x1, waiting for transfers between devices, local(): lax.all_gather(up_factors.astype(jnp.bfloat16), ('dp', 'role'), axis=0, t...  26 us
    all_gather x1, waiting for transfers between devices, local(): lax.all_gather(fresh_down, ('dp', 'role'), axis=0, tiled=True)  25.7 us
    convert_element_type x1, other arithmetic, dequantize(): return (base_weight.astype(jnp.float32) * spread).astype(jnp.bfloat16)  23.7 us
    unnamed x1, matrix products  18.2 us
  transfers between devices with their start and end apart: 9, of which 7 were waited for; matrix products, arithmetic and copies ran while one was open for 13% of the time, Pallas kernels for 0%

commit v1 on v0

v1 whole, which is shorter than its diff:
```python
import functools
import math

import jax
import jax.numpy as jnp
from jax import lax
from jax.experimental import pallas as pl
from jax.experimental.pallas import tpu as pltpu
from jax.sharding import PartitionSpec as P

HEAD_DIM = 128
ADAPTER_RANK = 32
GROUP = 64
BLOCK = 128
CHUNKS = 4

ADAPTER_SCALE = 2.0
FIRST_DECAY = 0.9
SECOND_DECAY = 0.999
FIRST_CORR = 1.0 / (1.0 - 0.9**10)
SECOND_CORR = 1.0 / (1.0 - 0.999**10)
ADAM_EPS = 1e-08
STEP_RATE = 0.002
BF16 = jnp.bfloat16
F32 = jnp.float32
SMALL = pl.CostEstimate(flops=1024, bytes_accessed=1024, transcendentals=0)


def moment_step_update(master, gradient, first, second):
    first_new = FIRST_DECAY * first + (1.0 - FIRST_DECAY) * gradient
    second_new = SECOND_DECAY * second + (1.0 - SECOND_DECAY) * gradient * gradient
    update = first_new * FIRST_CORR / (jnp.sqrt(second_new * SECOND_CORR) + ADAM_EPS)
    return (update, master - STEP_RATE * update)


def attend(query_vector, kv_cache, new_kv, cache_len):
    row_count = query_vector.shape[0]
    heads_kv = kv_cache.shape[1]
    positions = kv_cache.shape[2]
    grouped = query_vector.reshape(row_count, heads_kv, -1, HEAD_DIM)
    keys = kv_cache[..., :HEAD_DIM]
    values = kv_cache[..., HEAD_DIM:]
    inverse = 1.0 / math.sqrt(HEAD_DIM)
    scores = jnp.einsum("bkgh,bkph->bkgp", grouped, keys, preferred_element_type=F32) * inverse
    own = (
        jnp.einsum("bkgh,bkh->bkg", grouped, new_kv[..., :HEAD_DIM], preferred_element_type=F32)
        * inverse
    )
    live = (jnp.arange(positions, dtype=jnp.int32)[None, :] < cache_len[:, None])[:, None, None, :]
    top = jnp.maximum(jnp.max(jnp.where(live, scores, -jnp.inf), axis=-1), own)
    expo = jnp.where(live, jnp.exp(scores - top[..., None]), 0.0)
    own_expo = jnp.exp(own - top)
    total = jnp.sum(expo, axis=-1) + own_expo
    weights = (expo / total[..., None]).astype(BF16)
    own_weight = (own_expo / total).astype(BF16)
    own_value = new_kv[..., HEAD_DIM:].astype(F32)
    mixed = jnp.einsum("bkgp,bkph->bkgh", weights, values, preferred_element_type=F32)
    mixed = mixed + own_weight.astype(F32)[..., None] * own_value[:, :, None, :]
    return mixed.astype(BF16).reshape(row_count, -1)


def bit_reversed(count):
    bits = count.bit_length() - 1
    return [int(format(i, "b").zfill(bits)[::-1], 2) if bits else 0 for i in range(count)]


def whole(shape):
    return pl.BlockSpec(shape, lambda *_: (0,) * len(shape))


def params(mib=40):
    return pltpu.CompilerParams(vmem_limit_bytes=mib * 2**20)


def pack(down, up, *more):
    parts = (down, up, *more)
    widths = [part.shape[1] for part in parts]

    def kernel(*refs):
        at = 0
        for ref, width in zip(refs, widths):
            refs[-1][:, at : at + width] = ref[...].astype(BF16)
            at += width

    return pl.pallas_call(
        kernel,
        out_shape=jax.ShapeDtypeStruct((down.shape[0], sum(widths)), BF16),
        compiler_params=params(),
        cost_estimate=SMALL,
    )(*parts)


def dequantize(base_weight, base_scale, y):
    rows, shard = base_weight.shape
    half = rows // CHUNKS // 2
    groups = half // GROUP
    scale = base_scale.reshape(2 * CHUNKS, groups, shard)

    def kernel(y_ref, weight_ref, scale_ref, out_ref, *pieces):
        spread = jnp.broadcast_to(
            scale_ref[0].astype(F32)[:, None, :], (groups, GROUP, shard)
        ).reshape(half, shard)
        value = (weight_ref[...].astype(F32) * spread).astype(BF16)
        out_ref[...] = value
        for k, piece in enumerate(pieces):

            @pl.when(pl.program_id(0) == 2 * k + y_ref[0])
            def _(piece=piece):
                piece[...] = value

    block = pl.BlockSpec((half, shard), lambda i, _: (i, 0))
    outs = pl.pallas_call(
        kernel,
        grid_spec=pltpu.PrefetchScalarGridSpec(
            num_scalar_prefetch=1,
            grid=(2 * CHUNKS,),
            in_specs=[block, pl.BlockSpec((1, groups, shard), lambda i, _: (i, 0, 0))],
            out_specs=[block] + [whole((half, shard))] * CHUNKS,
        ),
        out_shape=[jax.ShapeDtypeStruct((rows, shard), BF16)]
        + [jax.ShapeDtypeStruct((half, shard), BF16)] * CHUNKS,
        compiler_params=params(),
        cost_estimate=SMALL,
    )(y.reshape(1), base_weight, scale)
    return outs[0], outs[1:]


def shares_of(value, x):
    rows, columns = value.shape

    def kernel(x_ref, first_ref, second_ref, first_out, second_out):
        first_out[...] = first_ref[...]
        second_out[...] = second_ref[...]

    shape = (rows, columns // 2)
    return pl.pallas_call(
        kernel,
        grid_spec=pltpu.PrefetchScalarGridSpec(
            num_scalar_prefetch=1,
            grid=(1,),
            in_specs=[
                pl.BlockSpec(shape, lambda i, x: (0, x[0])),
                pl.BlockSpec(shape, lambda i, x: (0, x[0] ^ 1)),
            ],
            out_specs=[whole(shape)] * 2,
        ),
        out_shape=[jax.ShapeDtypeStruct(shape, value.dtype)] * 2,
        compiler_params=params(),
        cost_estimate=SMALL,
    )(x.reshape(1), value, value)


def arrange_kernel(shard, place, first_ref, second_ref, out_ref):
    x, near, core = place[0], place[1], place[2]
    for j in range(4):
        share, column = near ^ (j // 2), core ^ (j % 2)
        lanes = pl.ds(pl.multiple_of(column * shard, shard), shard)

        @pl.when(share == x)
        def _(j=j, lanes=lanes):
            out_ref[:, j * shard : (j + 1) * shard] = first_ref[:, lanes]

        @pl.when(share != x)
        def _(j=j, lanes=lanes):
            out_ref[:, j * shard : (j + 1) * shard] = second_ref[:, lanes]


def arrange(first, second, shard, place):
    rows, share = first.shape
    return pl.pallas_call(
        functools.partial(arrange_kernel, shard),
        grid_spec=pltpu.PrefetchScalarGridSpec(
            num_scalar_prefetch=1,
            grid=(1,),
            in_specs=[whole((rows, share))] * 2,
            out_specs=whole((rows, 2 * share)),
        ),
        out_shape=jax.ShapeDtypeStruct((rows, 2 * share), BF16),
        compiler_params=params(),
        cost_estimate=SMALL,
    )(place, first, second)


def project(parts, pick, x_in, cot, width, blocks):
    owned, total = parts[0].shape
    model = x_in.shape[1]
    count = len(parts)

    def kernel(pick_ref, x_ref, cot_ref, *refs):
        table_ref, low_ref, rest_ref, every = refs[count:]
        for i, ref in enumerate(refs[:count]):
            every[i * owned : (i + 1) * owned] = ref[:, :width]
            rest_ref[i * owned : (i + 1) * owned] = ref[:, width:]
        table_ref[...] = jnp.dot(
            pick_ref[...], every[...], preferred_element_type=F32
        ).astype(BF16)
        for b in range(blocks):
            tokens = slice(b * BLOCK, (b + 1) * BLOCK)
            ranks = slice(b * ADAPTER_RANK, (b + 1) * ADAPTER_RANK)
            low_ref[tokens, :ADAPTER_RANK] = lax.dot_general(
                x_ref[tokens],
                table_ref[ranks, :model],
                (((1,), (1,)), ((), ())),
                preferred_element_type=F32,
            )
            low_ref[tokens, ADAPTER_RANK:] = lax.dot_general(
                cot_ref[tokens],
                table_ref[ranks, model:],
                (((1,), (1,)), ((), ())),
                preferred_element_type=F32,
            )

    return pl.pallas_call(
        kernel,
        out_shape=[
            jax.ShapeDtypeStruct((blocks * ADAPTER_RANK, width), BF16),
            jax.ShapeDtypeStruct((x_in.shape[0], 2 * ADAPTER_RANK), F32),
            jax.ShapeDtypeStruct((count * owned, total - width), BF16),
        ],
        scratch_shapes=[pltpu.VMEM((count * owned, width), BF16)],
        compiler_params=params(),
        cost_estimate=SMALL,
    )(pick, x_in, cot, *parts)


def factor_gradients(low, rank_of, belongs, x_in, cot):
    slots = rank_of.shape[1]
    half = slots // 2
    model, width = x_in.shape[1], x_in.shape[1] + cot.shape[1]

    def kernel(low_ref, rank_ref, belongs_ref, x_ref, cot_ref, keep_ref, send_ref):
        for at, source, ranks in (
            (0, x_ref, slice(ADAPTER_RANK, 2 * ADAPTER_RANK)),
            (model, cot_ref, slice(0, ADAPTER_RANK)),
        ):
            wide = jnp.dot(low_ref[:, ranks], rank_ref[...], preferred_element_type=F32)
            wide = (wide * belongs_ref[...]).astype(BF16)
            columns = source.shape[1]
            for first in range(0, columns, 512):
                size = min(512, columns - first)
                product = lax.dot_general(
                    wide,
                    source[:, first : first + size],
                    (((0,), (0,)), ((), ())),
                    preferred_element_type=F32,
                )
                lanes = slice(at + first, at + first + size)
                keep_ref[:, lanes] = product[:half]
                send_ref[:, lanes] = product[half:].astype(BF16)

    return pl.pallas_call(
        kernel,
        out_shape=[
            jax.ShapeDtypeStruct((half, width), F32),
            jax.ShapeDtypeStruct((half, width), BF16),
        ],
        compiler_params=params(),
        cost_estimate=SMALL,
    )(low, rank_of, belongs, x_in, cot)


def through_weight(cot, weight, weight_core, near, chunk, y, adapter=None):
    tokens = cot.shape[0]
    half, shard = near[0].shape
    rows = 2 * half

    def kernel(y_ref, cot_ref, own_ref, core_ref, mine, other, mine_core, other_core, *refs):
        out_ref = refs[-1]

        def run(near_ref, near_core_ref):
            total = None
            for j, ref in enumerate((own_ref, core_ref, near_ref, near_core_ref)):
                term = lax.dot_general(
                    cot_ref[:, j * shard : (j + 1) * shard],
                    ref[...],
                    (((1,), (1,)), ((), ())),
                    preferred_element_type=F32,
                )
                total = term if total is None else total + term
            if adapter is not None:
                total = total + ADAPTER_SCALE * jnp.dot(
                    refs[0][...], refs[1][...], preferred_element_type=F32
                )
            out_ref[...] = total.astype(out_ref.dtype)

        @pl.when(pl.program_id(0) == y_ref[0])
        def _():
            run(mine, mine_core)

        @pl.when(pl.program_id(0) != y_ref[0])
        def _():
            run(other, other_core)

    block = pl.BlockSpec((half, shard), lambda i, _: (2 * chunk + i, 0))
    operands = [cot, weight, weight_core, *near]
    specs = [whole(cot.shape), block, block] + [whole((half, shard))] * 4
    if adapter is not None:
        low, table = adapter
        operands += [low, table]
        specs += [
            whole(low.shape),
            pl.BlockSpec((table.shape[0], half), lambda i, _: (0, 2 * chunk + i)),
        ]
    dtype = BF16 if adapter is None else F32
    return pl.pallas_call(
        kernel,
        grid_spec=pltpu.PrefetchScalarGridSpec(
            num_scalar_prefetch=1,
            grid=(2,),
            in_specs=specs,
            out_specs=pl.BlockSpec((tokens, half), lambda i, _: (0, i)),
        ),
        out_shape=jax.ShapeDtypeStruct((tokens, rows), dtype),
        compiler_params=params(),
        cost_estimate=SMALL,
    )(y.reshape(1), *operands)


def final_kernel(count, own_ref, *refs):
    away, out_ref = refs[:count], refs[-1]
    total = own_ref[...]
    for part in away:
        total = total + part[...].astype(F32)
    out_ref[...] = total.astype(BF16)


def finish(own, away, out, chunk, model):
    tokens, rows = own.shape
    operands = [own, *away]
    specs = [whole(own.shape)] + [whole(part.shape) for part in away]
    aliases = {}
    if out is not None:
        aliases = {len(operands): 0}
        operands.append(out)
        specs.append(pl.BlockSpec(memory_space=pl.ANY))
    return pl.pallas_call(
        functools.partial(final_kernel, len(away)),
        grid=(1,),
        in_specs=specs,
        out_specs=pl.BlockSpec((tokens, rows), lambda i: (0, chunk)),
        out_shape=jax.ShapeDtypeStruct((tokens, model), BF16),
        input_output_aliases=aliases,
        compiler_params=params(),
        cost_estimate=SMALL,
    )(*operands)


def local(sizes, *arguments):
    (
        train_x,
        train_cot,
        tenant_of_block,
        down_factors,
        up_factors,
        down_mean_moment,
        down_square_moment,
        up_mean_moment,
        up_square_moment,
        base_weight,
        base_scale,
        row_hidden,
        row_tenant,
        cache_len,
        kv_cache,
        new_kv,
    ) = arguments
    depth, cores, halves = sizes["dp"], sizes["role"], sizes["mp"]
    y, z = lax.axis_index("groups"), lax.axis_index("dp")
    x, core = lax.axis_index("mp"), lax.axis_index("role")
    token_rows, model_local = train_x.shape
    query_local = train_cot.shape[1]
    block_count = token_rows // BLOCK
    owned = down_factors.shape[0]
    shard = base_weight.shape[1]
    order = bit_reversed(depth)

    def swap(value, axis, mask=1):
        return lax.ppermute(value, axis, [(i, i ^ mask) for i in range(sizes[axis])])

    def total_mp(value):
        mask = 1
        while mask < halves:
            value = value + swap(value, "mp", mask)
            mask *= 2
        return value

    def after(value, *others):
        return lax.optimization_barrier((value, others))[0]

    last = [None]

    def joint(*values):
        behind = () if last[0] is None else (last[0],)
        out = lax.optimization_barrier((*values, *behind))[: len(values)]
        last[0] = out[0]
        return out

    def mark(value):
        last[0] = value
        return value

    rows_own = row_hidden.shape[0]
    hidden_width = rows_own * model_local // owned
    hidden_own = lax.dynamic_slice_in_dim(row_hidden, x * model_local, model_local, 1)
    factors = pack(
        down_factors,
        up_factors,
        hidden_own.reshape(owned, hidden_width),
        jnp.broadcast_to(
            jnp.pad(row_tenant.astype(BF16), (0, 128 - rows_own))[None, :], (owned, 128)
        ),
    )
    far = swap(factors, "dp", depth // 2)
    early = swap(factors, "dp", depth // 4)
    held = {0: factors, depth // 2: far}
    first, second = shares_of(train_cot, x) if halves == 2 else (factors, factors)
    mines, others = [None] * CHUNKS, [None] * CHUNKS

    assert depth == 2 * halves and query_local == 2 * cores * shard
    pair = z // 2
    away_masks = list(range(2, depth, 2))

    def wide_cotangents():
        every = lax.all_gather(train_cot, "mp", axis=1, tiled=True)

        def columns(value, base):
            return jnp.concatenate(
                [
                    lax.dynamic_slice_in_dim(value, (zz * cores + cc) * shard - base, shard, 1)
                    for zz in (z, z ^ 1)
                    for cc in (core, core ^ 1)
                ],
                axis=1,
            )

        found = [columns(every, 0)]
        for mask in away_masks:
            wanted = (pair ^ (mask // 2)) * query_local
            got = swap(lax.dynamic_slice_in_dim(every, wanted, query_local, 1), "dp", mask)
            found.append(columns(got, pair * query_local))
        return found

    mask = depth // 4
    if halves == 2:
        near_first = swap(second, "mp")
        weight, pieces = dequantize(after(base_weight, near_first), base_scale, y)
        far, near_first, early, weight = joint(far, near_first, early, weight)
        far_cot = swap(jnp.where(x == pair, near_first, first), "dp", 2)
    else:
        cot_own, *cot_away = wide_cotangents()
        weight, pieces = dequantize(base_weight, base_scale, y)
        far, early, weight = joint(far, early, weight)
        far_cot = far

    weight_core = swap(weight, "role")
    mines[0] = swap(pieces[0], "dp", 1)

    held[depth // 2] = far
    while mask:
        for slot in list(held):
            given = mask == depth // 4 and slot == 0
            held[slot ^ mask] = early if given else swap(held[slot], "dp", mask)
        mask //= 2
    zl = after(z, far)
    tenants = after(tenant_of_block, far)
    slots = jnp.array(order, jnp.int32)
    owners = jnp.concatenate([(zl ^ slots) * cores + core, (zl ^ slots) * cores + (core ^ 1)])
    row_ids = (owners[:, None] * owned + jnp.arange(owned, dtype=jnp.int32)[None, :]).reshape(-1)
    wanted = tenants[:, None] * ADAPTER_RANK + jnp.arange(ADAPTER_RANK, dtype=jnp.int32)
    pick = (wanted.reshape(-1)[:, None] == row_ids[None, :]).astype(BF16)
    rank_of = (
        jnp.arange(ADAPTER_RANK, dtype=jnp.int32)[:, None] == (row_ids % ADAPTER_RANK)[None, :]
    ).astype(BF16)
    token_tenant = jnp.repeat(tenants, BLOCK)
    belongs = (token_tenant[:, None] == (row_ids // ADAPTER_RANK)[None, :]).astype(F32)

    mine = [held[slot] for slot in order]
    mine_cores, other_cores = [None] * CHUNKS, [None] * CHUNKS

    def fetch(k):
        mines[k] = swap(after(pieces[k], last[0]), "dp", 1)

    def to_core(value, *behind):
        return swap(after(value, *behind) if behind else value, "role")

    width = model_local + query_local
    count = len(mine)
    own_near = swap(mine[0], "role")
    far_cot, mines[0], weight_core, own_near, *found = joint(
        far_cot, mines[0], weight_core, own_near, *mine
    )
    far_cot_near = swap(far_cot, "mp") if halves == 2 else far_cot
    others[0] = swap(mines[0], "groups")
    fetch(1)
    parts = joint(*found, own_near, *[swap(part, "role") for part in found[1:]])
    table, low_terms, beside = project(parts, pick, train_x, train_cot, width, block_count)
    low_sum = total_mp(mark(low_terms))
    hidden = beside[:, :hidden_width].reshape(-1, model_local)
    hidden_tenant = beside[:, hidden_width:].reshape(-1, owned, 128)[:, 0, :rows_own]
    hidden_tenant = hidden_tenant.reshape(-1)

    low_sum, mine_cores[0], other_cores[0], mine_cores[1] = joint(
        low_sum,
        to_core(mines[0], far_cot_near, low_terms),
        to_core(others[0], low_terms),
        to_core(mines[1], low_terms),
    )
    fetch(2)
    low = low_sum.astype(BF16)
    keep, give = factor_gradients(low, rank_of, belongs, train_x, train_cot)
    got = swap(mark(give), "role")
    if halves == 2:
        place = jnp.stack([x, z % 2, core])
        cot_away = [mark(arrange(far_cot, after(far_cot_near, give), shard, place))]

    sent, arrived = [None] * CHUNKS, [None] * CHUNKS

    def partial(k, behind):
        near = (mines[k], others[k], mine_cores[k], other_cores[k])
        sent[k] = [
            through_weight(after(cot, behind), weight, weight_core, near, k, y)
            for cot in cot_away
        ]

    def send(k):
        arrived[k] = [swap(value, "dp", mask) for value, mask in zip(sent[k], away_masks)]

    def echo(value):
        return swap(value[:16, :128], "role")

    def stage(value, axis, mask, dtype):
        half = value.shape[0] // 2
        sent = mark(value[half:].astype(dtype))
        return value[:half], swap(sent, axis, mask)

    def settle(kept, got):
        return kept.astype(F32) + after(got, last[0]).astype(F32)

    masks = [1 << i for i in range(depth.bit_length() - 1)]
    partial(0, give)
    send(0)
    got, mines[2], *sent[0] = joint(got, mines[2], *sent[0])
    others[1] = swap(mines[1], "groups")
    kept, got = stage(settle(keep, got), "dp", masks[0], BF16)
    other_cores[1] = to_core(others[1])
    partial(1, give)
    send(1)
    far_second = swap(after(first, give), "mp") if halves == 2 else got
    mine_cores[2] = to_core(
        mines[2], got, echo(arrived[0][0]), far_second, sent[1][0]
    )
    got, mine_cores[2], far_second, *rest = joint(
        got, mine_cores[2], far_second, *arrived[0], *sent[1]
    )
    arrived[0] = rest[: len(sent[1])]
    others[2] = swap(mines[2], "groups")
    fetch(3)
    for mask in masks[1:]:
        kept, got = stage(settle(kept, got), "dp", mask, BF16)
    other_cores[2] = to_core(others[2])
    partial(2, got if depth > 4 else give)
    send(2)
    base_query = jnp.dot(after(hidden, sent[1][0]), weight, preferred_element_type=F32)
    mine_cores[3] = to_core(
        mines[3], got, echo(arrived[1][0]), sent[2][0], base_query
    )
    got, mine_cores[3], base_query, *rest = joint(
        got, mine_cores[3], base_query, *arrived[1], *sent[2]
    )
    arrived[1] = rest[: len(sent[2])]
    others[3] = swap(mines[3], "groups")
    other_cores[3] = to_core(others[3])
    partial(3, mine_cores[3])

    gradient = settle(kept, got)
    down_direction, revised_down = moment_step_update(
        down_factors,
        ADAPTER_SCALE * gradient[:, :model_local],
        down_mean_moment,
        down_square_moment,
    )
    up_direction, revised_up = moment_step_update(
        up_factors, ADAPTER_SCALE * gradient[:, model_local:], up_mean_moment, up_square_moment
    )
    fresh_down, fresh_up = revised_down.astype(BF16), revised_up.astype(BF16)

    rank_terms = lax.dot_general(
        hidden, fresh_down, (((1,), (1,)), ((), ())), preferred_element_type=F32
    )
    both = total_mp(
        jnp.concatenate(
            [base_query, jnp.pad(rank_terms, ((0, 0), (0, -rank_terms.shape[1] % 128)))], axis=1
        )
    )
    base_query, rank_terms = both[:, :shard], both[:, shard : shard + owned]
    first_col = (z * cores + core) * shard
    placed = lax.dynamic_update_slice(
        jnp.zeros((hidden.shape[0], query_local), F32),
        base_query,
        (0, first_col % query_local),
    )
    placed = jnp.where(x == first_col // query_local, placed, 0.0)
    my_tenant = ((z * cores + core) * owned + jnp.arange(owned, dtype=jnp.int32)) // ADAPTER_RANK
    row_low = jnp.where(
        hidden_tenant.astype(jnp.int32)[:, None] == my_tenant[None, :], rank_terms, 0.0
    ).astype(BF16)
    delta = jnp.dot(row_low, fresh_up, preferred_element_type=F32)
    query = placed + ADAPTER_SCALE * delta
    half = query.shape[0] // 2
    kept, got = query[:half], swap(after(query[half:], echo(arrived[2][0]), sent[3][0]), "role")
    got, *rest = joint(got, *arrived[2], *sent[3])
    arrived[2], sent[3] = rest[: len(sent[3])], rest[len(sent[3]) :]
    send(3)
    for mask in masks:
        kept, got = stage(settle(kept, got), "dp", mask, F32)

    block_of = jnp.repeat(jnp.arange(block_count, dtype=jnp.int32), BLOCK)
    col_block = jnp.repeat(jnp.arange(block_count, dtype=jnp.int32), ADAPTER_RANK)
    low_blocks = jnp.where(
        block_of[:, None] == col_block[None, :],
        jnp.tile(low[:, ADAPTER_RANK:], (1, block_count)),
        0,
    ).astype(BF16)
    if halves == 2:
        cot_own = arrange(
            jnp.where(x == pair, first, near_first),
            jnp.where(x == pair, second, far_second),
            shard,
            place,
        )
    owns = []
    for k in range(CHUNKS):
        near = (mines[k], others[k], mine_cores[k], other_cores[k])
        owns.append(
            through_weight(cot_own, weight, weight_core, near, k, y, adapter=(low_blocks, table))
        )
    out = None
    for k in range(CHUNKS - 1):
        out = finish(owns[k], arrived[k], out, k, model_local)
    got, out, owns[-1], *arrived[-1] = joint(got, out, owns[-1], *arrived[-1])
    out = finish(owns[-1], arrived[-1], out, CHUNKS - 1, model_local)
    query = settle(kept, got).astype(BF16)
    attended = attend(query, kv_cache, new_kv, cache_len)
    return (down_direction, up_direction, out, attended)


def solution(mesh):
    rows = ("groups", "dp", "role")
    in_specs = (
        P(rows, "mp"),
        P(rows, "mp"),
        P(rows),
        P(rows, "mp"),
        P(rows, "mp"),
        P(rows, "mp"),
        P(rows, "mp"),
        P(rows, "mp"),
        P(rows, "mp"),
        P("mp", ("dp", "role")),
        P("mp", ("dp", "role")),
        P(rows, None),
        P(rows),
        P(rows),
        P(rows, "mp", None, None),
        P(rows, "mp", None),
    )
    out_specs = (P(rows, "mp"), P(rows, "mp"), P(rows, "mp"), P(rows, "mp"))
    sizes = dict(mesh.shape)
    return jax.shard_map(
        functools.partial(local, sizes),
        mesh=mesh,
        in_specs=in_specs,
        out_specs=out_specs,
        check_vma=False,
    )
```

time: 617 us -> 250 us (0.41)
  waiting for transfers between devices: 457 us -> 115 us
  matrix products: 64.4 us -> 7.82 us
  Pallas kernels: 0 us -> 43.9 us
  starting transfers between devices: 0.54 us -> 35.7 us
  blocking collectives: 32.5 us -> 0 us
  other arithmetic: 30.3 us -> 10.5 us
  local copies, waits for them, and re-layouts: 17.7 us -> 34.3 us
  between operations: 14 us -> 1.48 us
    all_gather x6 -> x0, waiting for transfers between devices: 362 us -> none  [the longest x1 284 us: local(): lax.all_gather(base_weight, ('dp', 'role'), axis=1, tiled=True)]
    ppermute x0 -> x40, waiting for transfers between devices: none -> 115 us  [swap(): lax.ppermute(value, axis, [(i, i ^ mask) for i in range(sizes[axis])])]
    reduce_scatter x2 -> x0, waiting for transfers between devices: 83.3 us -> none  [the longest x1 48.8 us: local(): lax.psum_scatter(dense_down, ('dp', 'role'), scatter_dimension=0, tiled=T...]
    pallas_call x0 -> x19, Pallas kernels: none -> 43.9 us  [the longest x8 25.5 us: through_weight(): pl.pallas_call(kernel, grid_spec=pltpu.PrefetchScalarGridSpec(num_scalar_...]
    dot_general x16 -> x5, matrix products: 46.1 us -> 7.69 us  [the longest x1 2.91 us: local(): jnp.dot(after(hidden, sent[1][0]), weight, preferred_element_type=F32)]
    ppermute x0 -> x40, starting transfers between devices: none -> 35.7 us  [swap(): lax.ppermute(value, axis, [(i, i ^ mask) for i in range(sizes[axis])])]
    convert_element_type x8, other arithmetic: 30 us -> 0.88 us  [the longest x1 0.66 us: local(): row_tenant.astype(BF16)]
    unnamed x30 -> x140, local copies, waits for them, and re-layouts: 4.49 us -> 26.2 us
  transfers between devices with their start and end apart: 9 -> 40, of which waited for: 7 -> 21; matrix products, arithmetic and copies ran while one was open for 13% -> 8% of each run, Pallas kernels for 0% -> 16%
where the time goes in v1:
time: 250 us; the launch traced here: 249 us
  waiting for transfers between devices  115 us (46%)
  Pallas kernels  43.9 us (18%)
  starting transfers between devices  35.7 us (14%)
  local copies, waits for them, and re-layouts  34.3 us (14%)
  other arithmetic  10.5 us (4%)
  matrix products  7.82 us (3%)
    ppermute x40, waiting for transfers between devices, swap(): lax.ppermute(value, axis, [(i, i ^ mask) for i in range(sizes[axis])])  115 us
    ppermute x40, starting transfers between devices, swap(): lax.ppermute(value, axis, [(i, i ^ mask) for i in range(sizes[axis])])  35.7 us
    unnamed x140, local copies, waits for them, and re-layouts  26.2 us
    pallas_call x8, Pallas kernels, through_weight(): pl.pallas_call(kernel, grid_spec=pltpu.PrefetchScalarGridSpec(num_scalar_...  25.5 us
    pallas_call x4, Pallas kernels, finish(): pl.pallas_call(functools.partial(final_kernel, len(away)), grid=(1,), in_...  5.7 us
  transfers between devices with their start and end apart: 40, of which 21 were waited for; matrix products, arithmetic and copies ran while one was open for 8% of the time, Pallas kernels for 16%

profile of v1, /device:TPU:0, one launch (start us, length us, event | category | flops | bytes accessed | tf_op | source)
XLA Modules:
  0.0 248.6 jit_solution(5227153644967209227)
XLA Ops:
  2.0 3.0 %collective-permute-start.1 = (bf16[256,1024]{1,0:T(8,128)(2,1)S(1)}, bf16[256,1024]{1,0:T(8,128)(2,1)S(1)}, u32[]{:S(2)}, u32[]{:S(2)}) collective-permute-start(bf16[256,1024]{1,0:T(8,128)(2,1)S(1)} %get-tuple-element.77), channel_id=1, source_target_pairs={{0,2},{2,0},{1,3},{3,1},{4,6},{6,4},{5,7},{7,5},{8,10},{10,8},{9,1... | collective-permute-start | bytes 1572872 | tf_op jit(solution)/shard_map/ppermute | solution.py:378
  12.0 4.9 %collective-permute-done.1 = bf16[256,1024]{1,0:T(8,128)(2,1)S(1)} collective-permute-done((bf16[256,1024]{1,0:T(8,128)(2,1)S(1)}, bf16[256,1024]{1,0:T(8,128)(2,1)S(1)}, u32[]{:S(2)}, u32[]{:S(2)}) %collective-permute-start.1) | collective-permute-done | bytes 524320 | tf_op jit(solution)/shard_map/ppermute | solution.py:378
  19.9 4.4 %shard_map.194 = (bf16[4096,512]{1,0:T(8,128)(2,1)}, bf16[512,512]{1,0:T(8,128)(2,1)S(1)}, bf16[512,512]{1,0:T(8,128)(2,1)S(1)}, bf16[512,512]{1,0:T(8,128)(2,1)}, bf16[512,512]{1,0:T(8,128)(2,1)}) custom-call(s32[1]{0:T(128)} %bitcast.1.y_ref, bf16[4096,512]{1,0:T(8,128)(2,1)S(1)} %copy-done.5, bf16[8,8,512]{2,1,0:T(8,128)(2,1)S(1)} %bitcast.22), custom_call_target="tpu_custom_call" | custom-call | flops 1024 | bytes 1024 | tf_op jit(solution)/shard_map/pallas_call | solution.py:112
  25.9 3.0 %collective-permute-done.refs_1_ = bf16[32,6528]{1,0:T(8,128)(2,1)} collective-permute-done((bf16[32,6528]{1,0:T(8,128)(2,1)S(1)}, bf16[32,6528]{1,0:T(8,128)(2,1)}, u32[]{:S(2)}, u32[]{:S(2)}) %collective-permute-start) | collective-permute-done | bytes 417824 | tf_op jit(solution)/shard_map/ppermute | solution.py:378
  36.3 13.6 %collective-permute-done.7.refs_3_ = bf16[32,6528]{1,0:T(8,128)(2,1)S(1)} collective-permute-done((bf16[32,6528]{1,0:T(8,128)(2,1)}, bf16[32,6528]{1,0:T(8,128)(2,1)S(1)}, u32[]{:S(2)}, u32[]{:S(2)}) %collective-permute-start.7) | collective-permute-done | bytes 417824 | tf_op jit(solution)/shard_map/ppermute | solution.py:378
  49.9 8.3 %collective-permute-done.3.first_ref = bf16[256,1024]{1,0:T(8,128)(2,1)} collective-permute-done((bf16[256,1024]{1,0:T(8,128)(2,1)S(1)}, bf16[256,1024]{1,0:T(8,128)(2,1)}, u32[]{:S(2)}, u32[]{:S(2)}) %collective-permute-start.3) | collective-permute-done | bytes 524320 | tf_op jit(solution)/shard_map/ppermute | solution.py:378
  58.2 5.6 %collective-permute-done.4.mine = bf16[512,512]{1,0:T(8,128)(2,1)S(1)} collective-permute-done((bf16[512,512]{1,0:T(8,128)(2,1)}, bf16[512,512]{1,0:T(8,128)(2,1)S(1)}, u32[]{:S(2)}, u32[]{:S(2)}) %collective-permute-start.4) | collective-permute-done | bytes 524320 | tf_op jit(solution)/shard_map/ppermute | solution.py:378
  82.2 4.0 %collective-permute-done.11 = f32[256,64]{1,0:T(8,128)S(1)} collective-permute-done((f32[256,64]{1,0:T(8,128)S(1)}, f32[256,64]{1,0:T(8,128)S(1)}, u32[]{:S(2)}, u32[]{:S(2)}) %collective-permute-start.11) | collective-permute-done | bytes 65568 | tf_op jit(solution)/shard_map/ppermute | solution.py:378
  98.5 3.1 %shard_map.198 = bf16[256,1024]{1,0:T(8,128)(2,1)S(1)} custom-call(s32[1]{0:T(128)} %bitcast.1.y_ref, bf16[256,2048]{1,0:T(8,128)(2,1)S(1)} %shard_map.197.cot_ref, bf16[4096,512]{1,0:T(8,128)(2,1)} %get-tuple-element.86.own_ref, bf16[4096,512]{1,0:T(8,128)(2,1)} %collective-permute-done.5.core_ref, bf16[512,512]{1,0:T(8,128)(2,1)S(1)} %collective-permute-done.4.mine, ...), custom_call_target="tpu_custom_call" | custom-call | flops 1024 | bytes 1024 | tf_op jit(solution)/shard_map/pallas_call | solution.py:305
  101.6 5.4 %collective-permute-done.19.mine = bf16[512,512]{1,0:T(8,128)(2,1)} collective-permute-done((bf16[512,512]{1,0:T(8,128)(2,1)}, bf16[512,512]{1,0:T(8,128)(2,1)}, u32[]{:S(2)}, u32[]{:S(2)}) %collective-permute-start.19) | collective-permute-done | bytes 524320 | tf_op jit(solution)/shard_map/ppermute | solution.py:378
  114.4 3.0 %shard_map.199 = bf16[256,1024]{1,0:T(8,128)(2,1)S(1)} custom-call(s32[1]{0:T(128)} %bitcast.1.y_ref, bf16[256,2048]{1,0:T(8,128)(2,1)S(1)} %shard_map.197.cot_ref, bf16[4096,512]{1,0:T(8,128)(2,1)} %get-tuple-element.86.own_ref, bf16[4096,512]{1,0:T(8,128)(2,1)} %collective-permute-done.5.core_ref, bf16[512,512]{1,0:T(8,128)(2,1)S(1)} %collective-permute-done.16.mine, ...), custom_call_target="tpu_custom_call" | custom-call | flops 1024 | bytes 1024 | tf_op jit(solution)/shard_map/pallas_call | solution.py:305
  118.7 6.0 %collective-permute-done.21 = bf16[256,1024]{1,0:T(8,128)(2,1)S(1)} collective-permute-done((bf16[256,1024]{1,0:T(8,128)(2,1)S(1)}, bf16[256,1024]{1,0:T(8,128)(2,1)S(1)}, u32[]{:S(2)}, u32[]{:S(2)}) %collective-permute-start.21) | collective-permute-done | bytes 524320 | tf_op jit(solution)/shard_map/ppermute | solution.py:378
  124.7 14.8 %collective-permute-done.20 = bf16[64,6144]{1,0:T(8,128)(2,1)S(1)} collective-permute-done((bf16[64,6144]{1,0:T(8,128)(2,1)S(1)}, bf16[64,6144]{1,0:T(8,128)(2,1)S(1)}, u32[]{:S(2)}, u32[]{:S(2)}) %collective-permute-start.20) | collective-permute-done | bytes 786464 | tf_op jit(solution)/shard_map/ppermute | solution.py:378
  152.5 2.9 %fusion.41 = f32[16,512]{1,0:T(8,128)S(1)} fusion(bf16[16,4096]{1,0:T(8,128)(2,1)} %reshape.186, bf16[4096,512]{1,0:T(8,128)(2,1)} %get-tuple-element.86.own_ref), kind=kOutput, calls=%fused_computation.88 | convolution fusion | flops 67108864 | bytes 4358144 | tf_op jit(solution)/shard_map/dot_general | solution.py:563
  155.4 3.1 %shard_map.200 = bf16[256,1024]{1,0:T(8,128)(2,1)S(1)} custom-call(s32[1]{0:T(128)} %bitcast.1.y_ref, bf16[256,2048]{1,0:T(8,128)(2,1)S(1)} %shard_map.197.cot_ref, bf16[4096,512]{1,0:T(8,128)(2,1)} %get-tuple-element.86.own_ref, bf16[4096,512]{1,0:T(8,128)(2,1)} %collective-permute-done.5.core_ref, bf16[512,512]{1,0:T(8,128)(2,1)} %collective-permute-done.19.mine, ...), custom_call_target="tpu_custom_call" | custom-call | flops 1024 | bytes 1024 | tf_op jit(solution)/shard_map/pallas_call | solution.py:305
  159.3 6.6 %collective-permute-done.26 = bf16[32,6144]{1,0:T(8,128)(2,1)} collective-permute-done((bf16[32,6144]{1,0:T(8,128)(2,1)}, bf16[32,6144]{1,0:T(8,128)(2,1)}, u32[]{:S(2)}, u32[]{:S(2)}) %collective-permute-start.26) | collective-permute-done | bytes 393248 | tf_op jit(solution)/shard_map/ppermute | solution.py:378
  166.0 5.7 %collective-permute-done.27.mine = bf16[512,512]{1,0:T(8,128)(2,1)} collective-permute-done((bf16[512,512]{1,0:T(8,128)(2,1)}, bf16[512,512]{1,0:T(8,128)(2,1)}, u32[]{:S(2)}, u32[]{:S(2)}) %collective-permute-start.27) | collective-permute-done | bytes 524320 | tf_op jit(solution)/shard_map/ppermute | solution.py:378
  173.5 26.1 %collective-permute-done.31.refs_0_ = bf16[256,1024]{1,0:T(8,128)(2,1)} collective-permute-done((bf16[256,1024]{1,0:T(8,128)(2,1)}, bf16[256,1024]{1,0:T(8,128)(2,1)}, u32[]{:S(2)}, u32[]{:S(2)}) %collective-permute-start.31) | collective-permute-done | bytes 524320 | tf_op jit(solution)/shard_map/ppermute | solution.py:378
  207.8 3.3 %shard_map.201 = bf16[256,1024]{1,0:T(8,128)(2,1)S(1)} custom-call(s32[1]{0:T(128)} %bitcast.1.y_ref, bf16[256,2048]{1,0:T(8,128)(2,1)S(1)} %shard_map.197.cot_ref, bf16[4096,512]{1,0:T(8,128)(2,1)} %get-tuple-element.86.own_ref, bf16[4096,512]{1,0:T(8,128)(2,1)} %collective-permute-done.5.core_ref, bf16[512,512]{1,0:T(8,128)(2,1)} %collective-permute-done.27.mine, ...), custom_call_target="tpu_custom_call" | custom-call | flops 1024 | bytes 1024 | tf_op jit(solution)/shard_map/pallas_call | solution.py:305
  220.0 3.2 %shard_map.205.own_ref = f32[256,1024]{1,0:T(8,128)S(1)} custom-call(s32[1]{0:T(128)} %bitcast.1.y_ref, bf16[256,2048]{1,0:T(8,128)(2,1)S(1)} %shard_map.202.cot_ref, bf16[4096,512]{1,0:T(8,128)(2,1)} %get-tuple-element.86.own_ref, bf16[4096,512]{1,0:T(8,128)(2,1)} %collective-permute-done.5.core_ref, bf16[512,512]{1,0:T(8,128)(2,1)S(1)} %collective-permute-done.4.mine, ...), custom_call_target="tpu_custom_call" | custom-call | flops 1024 | bytes 1024 | tf_op jit(solution)/shard_map/pallas_call | solution.py:305
  224.6 3.5 %shard_map.203.own_ref = f32[256,1024]{1,0:T(8,128)S(1)} custom-call(s32[1]{0:T(128)} %bitcast.1.y_ref, bf16[256,2048]{1,0:T(8,128)(2,1)S(1)} %shard_map.202.cot_ref, bf16[4096,512]{1,0:T(8,128)(2,1)} %get-tuple-element.86.own_ref, bf16[4096,512]{1,0:T(8,128)(2,1)} %collective-permute-done.5.core_ref, bf16[512,512]{1,0:T(8,128)(2,1)} %collective-permute-done.19.mine, ...), custom_call_target="tpu_custom_call" | custom-call | flops 1024 | bytes 1024 | tf_op jit(solution)/shard_map/pallas_call | solution.py:305
  228.1 3.0 %shard_map.204.own_ref = f32[256,1024]{1,0:T(8,128)S(1)} custom-call(s32[1]{0:T(128)} %bitcast.1.y_ref, bf16[256,2048]{1,0:T(8,128)(2,1)S(1)} %shard_map.202.cot_ref, bf16[4096,512]{1,0:T(8,128)(2,1)} %get-tuple-element.86.own_ref, bf16[4096,512]{1,0:T(8,128)(2,1)} %collective-permute-done.5.core_ref, bf16[512,512]{1,0:T(8,128)(2,1)S(1)} %copy-done.11, ...), custom_call_target="tpu_custom_call" | custom-call | flops 1024 | bytes 1024 | tf_op jit(solution)/shard_map/pallas_call | solution.py:305
  233.2 3.3 %shard_map.209.own_ref = f32[256,1024]{1,0:T(8,128)S(1)} custom-call(s32[1]{0:T(128)} %bitcast.1.y_ref, bf16[256,2048]{1,0:T(8,128)(2,1)S(1)} %shard_map.202.cot_ref, bf16[4096,512]{1,0:T(8,128)(2,1)} %get-tuple-element.86.own_ref, bf16[4096,512]{1,0:T(8,128)(2,1)} %collective-permute-done.5.core_ref, bf16[512,512]{1,0:T(8,128)(2,1)} %collective-permute-done.27.mine, ...), custom_call_target="tpu_custom_call" | custom-call | flops 1024 | bytes 1024 | tf_op jit(solution)/shard_map/pallas_call | solution.py:305
  238.4 3.0 %collective-permute-done.38 = f32[2,2048]{1,0:T(2,128)S(1)} collective-permute-done((f32[2,2048]{1,0:T(2,128)S(1)}, f32[2,2048]{1,0:T(2,128)S(1)}, u32[]{:S(2)}, u32[]{:S(2)}) %collective-permute-start.38) | collective-permute-done | bytes 16416 | tf_op jit(solution)/shard_map/ppermute | solution.py:378
  (280 shorter events, 104.0 us)
Async XLA Ops:
  2.0 14.9 %collective-permute-start.1 = (bf16[256,1024]{1,0:T(8,128)(2,1)S(1)}, bf16[256,1024]{1,0:T(8,128)(2,1)S(1)}, u32[]{:S(2)}, u32[]{:S(2)}) collective-permute-start(bf16[256,1024]{1,0:T(8,128)(2,1)S(1)} %get-tuple-element.77), channel_id=1, source_target_pairs={{0,2},{2,0},{1,3},{3,1},{4,6},{6,4},{5,7},{7,5},{8,10},{10,8},{9,1... | collective-permute-start | bytes 1572872 | tf_op jit(solution)/shard_map/ppermute | solution.py:378
  7.7 21.2 %collective-permute-start = (bf16[32,6528]{1,0:T(8,128)(2,1)S(1)}, bf16[32,6528]{1,0:T(8,128)(2,1)}, u32[]{:S(2)}, u32[]{:S(2)}) collective-permute-start(bf16[32,6528]{1,0:T(8,128)(2,1)S(1)} %shard_map.192.refs_0_), channel_id=1, source_target_pairs={{0,8},{4,12},{8,0},{12,4},{1,9},{5,13},{9,1},{13,5},{2,10},{6,14},... | collective-permute-start | bytes 1253384 | tf_op jit(solution)/shard_map/ppermute | solution.py:378
  10.4 18.7 %collective-permute-start.2 = (bf16[32,6528]{1,0:T(8,128)(2,1)S(1)}, bf16[32,6528]{1,0:T(8,128)(2,1)S(1)}, u32[]{:S(2)}, u32[]{:S(2)}) collective-permute-start(bf16[32,6528]{1,0:T(8,128)(2,1)S(1)} %shard_map.192.refs_0_), channel_id=1, source_target_pairs={{0,4},{4,0},{8,12},{12,8},{1,5},{5,1},{9,13},{13,9},{2,6},{6,2},{1... | collective-permute-start | bytes 1253384 | tf_op jit(solution)/shard_map/ppermute | solution.py:378
  29.1 34.7 %collective-permute-start.5 = (bf16[4096,512]{1,0:T(8,128)(2,1)}, bf16[4096,512]{1,0:T(8,128)(2,1)}, u32[]{:S(2)}, u32[]{:S(2)}) collective-permute-start(bf16[4096,512]{1,0:T(8,128)(2,1)} %get-tuple-element.86.own_ref), channel_id=1, source_target_pairs={{0,1},{1,0},{2,3},{3,2},{4,5},{5,4},{6,7},{7,6},{8,9},{9,8},{10,11... | collective-permute-start | bytes 12582920 | tf_op jit(solution)/shard_map/ppermute | solution.py:378
  29.6 20.3 %collective-permute-start.7 = (bf16[32,6528]{1,0:T(8,128)(2,1)}, bf16[32,6528]{1,0:T(8,128)(2,1)S(1)}, u32[]{:S(2)}, u32[]{:S(2)}) collective-permute-start(bf16[32,6528]{1,0:T(8,128)(2,1)} %collective-permute-done.refs_1_), channel_id=1, source_target_pairs={{0,4},{4,0},{8,12},{12,8},{1,5},{5,1},{9,13},{13,9},{2,6},{6,2},{1... | collective-permute-start | bytes 1253384 | tf_op jit(solution)/shard_map/ppermute | solution.py:378
  32.2 26.0 %collective-permute-start.3 = (bf16[256,1024]{1,0:T(8,128)(2,1)S(1)}, bf16[256,1024]{1,0:T(8,128)(2,1)}, u32[]{:S(2)}, u32[]{:S(2)}) collective-permute-start(bf16[256,1024]{1,0:T(8,128)(2,1)S(1)} %get-tuple-element.151), channel_id=1, source_target_pairs={{0,8},{4,12},{8,0},{12,4},{1,9},{5,13},{9,1},{13,5},{2,10},{6,14},... | collective-permute-start | bytes 1572872 | tf_op jit(solution)/shard_map/ppermute | solution.py:378
  34.6 29.2 %collective-permute-start.4 = (bf16[512,512]{1,0:T(8,128)(2,1)}, bf16[512,512]{1,0:T(8,128)(2,1)S(1)}, u32[]{:S(2)}, u32[]{:S(2)}) collective-permute-start(bf16[512,512]{1,0:T(8,128)(2,1)} %copy-done.56), channel_id=1, source_target_pairs={{0,4},{4,0},{8,12},{12,8},{1,5},{5,1},{9,13},{13,9},{2,6},{6,2},{1... | collective-permute-start | bytes 1572872 | tf_op jit(solution)/shard_map/ppermute | solution.py:378
  63.8 15.7 %collective-permute-start.12 = (bf16[256,1024]{1,0:T(8,128)(2,1)}, bf16[256,1024]{1,0:T(8,128)(2,1)}, u32[]{:S(2)}, u32[]{:S(2)}) collective-permute-start(bf16[256,1024]{1,0:T(8,128)(2,1)} %collective-permute-done.3.first_ref), channel_id=1, source_target_pairs={{0,2},{2,0},{1,3},{3,1},{4,6},{6,4},{5,7},{7,5},{8,10},{10,8},{9,1... | collective-permute-start | bytes 1572872 | tf_op jit(solution)/shard_map/ppermute | solution.py:378
  64.4 15.6 %collective-permute-start.14 = (bf16[512,512]{1,0:T(8,128)(2,1)S(1)}, bf16[512,512]{1,0:T(8,128)(2,1)}, u32[]{:S(2)}, u32[]{:S(2)}) collective-permute-start(bf16[512,512]{1,0:T(8,128)(2,1)S(1)} %collective-permute-done.4.mine), channel_id=1, source_target_pairs={{0,16},{16,0},{1,17},{17,1},{2,18},{18,2},{3,19},{19,3},{4,20},{20... | collective-permute-start | bytes 1572872 | tf_op jit(solution)/shard_map/ppermute | solution.py:378
  92.4 14.7 %collective-permute-start.18 = (bf16[128,6144]{1,0:T(8,128)(2,1)}, bf16[128,6144]{1,0:T(8,128)(2,1)}, u32[]{:S(2)}, u32[]{:S(2)}) collective-permute-start(bf16[128,6144]{1,0:T(8,128)(2,1)} %get-tuple-element.111), channel_id=1, source_target_pairs={{0,1},{1,0},{2,3},{3,2},{4,5},{5,4},{6,7},{7,6},{8,9},{9,8},{10,11... | collective-permute-start | bytes 4718600 | tf_op jit(solution)/shard_map/ppermute | solution.py:378
  92.4 14.7 %collective-permute-start.19 = (bf16[512,512]{1,0:T(8,128)(2,1)}, bf16[512,512]{1,0:T(8,128)(2,1)}, u32[]{:S(2)}, u32[]{:S(2)}) collective-permute-start(bf16[512,512]{1,0:T(8,128)(2,1)} %get-tuple-element.113), channel_id=1, source_target_pairs={{0,4},{4,0},{8,12},{12,8},{1,5},{5,1},{9,13},{13,9},{2,6},{6,2},{1... | collective-permute-start | bytes 1572872 | tf_op jit(solution)/shard_map/ppermute | solution.py:378
  93.7 16.6 %collective-permute-start.22 = (bf16[512,512]{1,0:T(8,128)(2,1)S(1)}, bf16[512,512]{1,0:T(8,128)(2,1)S(1)}, u32[]{:S(2)}, u32[]{:S(2)}) collective-permute-start(bf16[512,512]{1,0:T(8,128)(2,1)S(1)} %collective-permute-done.16.mine), channel_id=1, source_target_pairs={{0,16},{16,0},{1,17},{17,1},{2,18},{18,2},{3,19},{19,3},{4,20},{20... | collective-permute-start | bytes 1572872 | tf_op jit(solution)/shard_map/ppermute | solution.py:378
  109.0 30.5 %collective-permute-start.20 = (bf16[64,6144]{1,0:T(8,128)(2,1)S(1)}, bf16[64,6144]{1,0:T(8,128)(2,1)S(1)}, u32[]{:S(2)}, u32[]{:S(2)}) collective-permute-start(bf16[64,6144]{1,0:T(8,128)(2,1)S(1)} %slice.141), channel_id=1, source_target_pairs={{0,4},{4,0},{8,12},{12,8},{1,5},{5,1},{9,13},{13,9},{2,6},{6,2},{1... | collective-permute-start | bytes 2359304 | tf_op jit(solution)/shard_map/ppermute | solution.py:378
  111.9 28.1 %collective-permute-start.25 = (bf16[256,1024]{1,0:T(8,128)(2,1)S(1)}, bf16[256,1024]{1,0:T(8,128)(2,1)S(1)}, u32[]{:S(2)}, u32[]{:S(2)}) collective-permute-start(bf16[256,1024]{1,0:T(8,128)(2,1)S(1)} %shard_map.198), channel_id=1, source_target_pairs={{0,8},{4,12},{8,0},{12,4},{1,9},{5,13},{9,1},{13,5},{2,10},{6,14},... | collective-permute-start | bytes 1572872 | tf_op jit(solution)/shard_map/ppermute | solution.py:378
  118.2 21.3 %collective-permute-start.28 = (bf16[512,512]{1,0:T(8,128)(2,1)}, bf16[512,512]{1,0:T(8,128)(2,1)S(1)}, u32[]{:S(2)}, u32[]{:S(2)}) collective-permute-start(bf16[512,512]{1,0:T(8,128)(2,1)} %collective-permute-done.19.mine), channel_id=1, source_target_pairs={{0,16},{16,0},{1,17},{17,1},{2,18},{18,2},{3,19},{19,3},{4,20},{20... | collective-permute-start | bytes 1572872 | tf_op jit(solution)/shard_map/ppermute | solution.py:378
  139.5 15.9 %collective-permute-start.29 = (bf16[512,512]{1,0:T(8,128)(2,1)S(1)}, bf16[512,512]{1,0:T(8,128)(2,1)}, u32[]{:S(2)}, u32[]{:S(2)}) collective-permute-start(bf16[512,512]{1,0:T(8,128)(2,1)S(1)} %collective-permute-done.28.other), channel_id=1, source_target_pairs={{0,1},{1,0},{2,3},{3,2},{4,5},{5,4},{6,7},{7,6},{8,9},{9,8},{10,11... | collective-permute-start | bytes 1572872 | tf_op jit(solution)/shard_map/ppermute | solution.py:378
  144.5 21.5 %collective-permute-start.26 = (bf16[32,6144]{1,0:T(8,128)(2,1)}, bf16[32,6144]{1,0:T(8,128)(2,1)}, u32[]{:S(2)}, u32[]{:S(2)}) collective-permute-start(bf16[32,6144]{1,0:T(8,128)(2,1)} %slice.142), channel_id=1, source_target_pairs={{0,8},{4,12},{8,0},{12,4},{1,9},{5,13},{9,1},{13,5},{2,10},{6,14},... | collective-permute-start | bytes 1179656 | tf_op jit(solution)/shard_map/ppermute | solution.py:378
  145.8 25.9 %collective-permute-start.27 = (bf16[512,512]{1,0:T(8,128)(2,1)}, bf16[512,512]{1,0:T(8,128)(2,1)}, u32[]{:S(2)}, u32[]{:S(2)}) collective-permute-start(bf16[512,512]{1,0:T(8,128)(2,1)} %get-tuple-element.127), channel_id=1, source_target_pairs={{0,4},{4,0},{8,12},{12,8},{1,5},{5,1},{9,13},{13,9},{2,6},{6,2},{1... | collective-permute-start | bytes 1572872 | tf_op jit(solution)/shard_map/ppermute | solution.py:378
  152.1 47.5 %collective-permute-start.31 = (bf16[256,1024]{1,0:T(8,128)(2,1)}, bf16[256,1024]{1,0:T(8,128)(2,1)}, u32[]{:S(2)}, u32[]{:S(2)}) collective-permute-start(bf16[256,1024]{1,0:T(8,128)(2,1)} %copy-done.42), channel_id=1, source_target_pairs={{0,8},{4,12},{8,0},{12,4},{1,9},{5,13},{9,1},{13,5},{2,10},{6,14},... | collective-permute-start | bytes 1572872 | tf_op jit(solution)/shard_map/ppermute | solution.py:378
  171.7 27.9 %collective-permute-start.30 = (bf16[512,512]{1,0:T(8,128)(2,1)}, bf16[512,512]{1,0:T(8,128)(2,1)}, u32[]{:S(2)}, u32[]{:S(2)}) collective-permute-start(bf16[512,512]{1,0:T(8,128)(2,1)} %collective-permute-done.27.mine), channel_id=1, source_target_pairs={{0,1},{1,0},{2,3},{3,2},{4,5},{5,4},{6,7},{7,6},{8,9},{9,8},{10,11... | collective-permute-start | bytes 1572872 | tf_op jit(solution)/shard_map/ppermute | solution.py:378
  172.7 39.3 %collective-permute-start.36 = (bf16[256,1024]{1,0:T(8,128)(2,1)}, bf16[256,1024]{1,0:T(8,128)(2,1)}, u32[]{:S(2)}, u32[]{:S(2)}) collective-permute-start(bf16[256,1024]{1,0:T(8,128)(2,1)} %copy-done.43), channel_id=1, source_target_pairs={{0,8},{4,12},{8,0},{12,4},{1,9},{5,13},{9,1},{13,5},{2,10},{6,14},... | collective-permute-start | bytes 1572872 | tf_op jit(solution)/shard_map/ppermute | solution.py:378
  172.8 31.7 %collective-permute-start.33 = (bf16[512,512]{1,0:T(8,128)(2,1)}, bf16[512,512]{1,0:T(8,128)(2,1)S(1)}, u32[]{:S(2)}, u32[]{:S(2)}) collective-permute-start(bf16[512,512]{1,0:T(8,128)(2,1)} %collective-permute-done.27.mine), channel_id=1, source_target_pairs={{0,16},{16,0},{1,17},{17,1},{2,18},{18,2},{3,19},{19,3},{4,20},{20... | collective-permute-start | bytes 1572872 | tf_op jit(solution)/shard_map/ppermute | solution.py:378
  214.6 26.9 %collective-permute-start.39 = (bf16[256,1024]{1,0:T(8,128)(2,1)S(1)}, bf16[256,1024]{1,0:T(8,128)(2,1)S(1)}, u32[]{:S(2)}, u32[]{:S(2)}) collective-permute-start(bf16[256,1024]{1,0:T(8,128)(2,1)S(1)} %shard_map.201), channel_id=1, source_target_pairs={{0,8},{4,12},{8,0},{12,4},{1,9},{5,13},{9,1},{13,5},{2,10},{6,14},... | collective-permute-start | bytes 1572872 | tf_op jit(solution)/shard_map/ppermute | solution.py:378
  217.7 23.7 %collective-permute-start.38 = (f32[2,2048]{1,0:T(2,128)S(1)}, f32[2,2048]{1,0:T(2,128)S(1)}, u32[]{:S(2)}, u32[]{:S(2)}) collective-permute-start(f32[2,2048]{1,0:T(2,128)S(1)} %slice.106), channel_id=1, source_target_pairs={{0,8},{4,12},{8,0},{12,4},{1,9},{5,13},{9,1},{13,5},{2,10},{6,14},... | collective-permute-start | bytes 49160 | tf_op jit(solution)/shard_map/ppermute | solution.py:378
  (86 other events, 754.6 us)
